TPU v7x, 256 devices: a whole 4x4x8 slice. The times are simulated.
256 devices in a mesh: replica: 8 (over y_lo, x), fsdp: 32 (over z, y_hi, core).
Axes of the slice: x: 4, y: 4 (y_hi: 2, y_lo: 2; y = y_hi * 2 + y_lo), z: 8, core: 2. Of those that a mesh axis runs over, the one named last changes fastest.
Arguments:
- embedded: bfloat16 [8, 12288, 8192], P('replica', 'fsdp'), may hold values from -6 to 6
- positions: int32 [8, 12288], P('replica', 'fsdp'), may hold values from 0 to 8191
- key_cotangent: bfloat16 [8, 12288, 512], P('replica', 'fsdp'), may hold values from -0.125 to 0.125
- local_weight: float32 [8, 8192, 512], P('replica', 'fsdp'), may hold values from -0.0625 to 0.0625
- adam_first: float32 [8, 8192, 512], P('replica', 'fsdp'), may hold values from -6 to 6
- adam_second: float32 [8, 8192, 512], P('replica', 'fsdp'), may hold values from 0.01 to 1
- pseudo_grad: float32 [8, 8192, 512], P('replica', 'fsdp'), may hold values from -0.00061035156 to 0.00061035156
- anchor: float32 [8192, 512], P('fsdp'), may hold values from -0.0625 to 0.0625
- momentum: float32 [8192, 512], P('fsdp'), may hold values from -0.00061035156 to 0.00061035156
Outputs:
- keys: bfloat16 [8, 12288, 512], P('replica', 'fsdp')
- merged: float32 [8, 8192, 512], P('replica', 'fsdp')
- new_first: float32 [8, 8192, 512], P('replica', 'fsdp')
- new_second: float32 [8, 8192, 512], P('replica', 'fsdp')
- new_anchor: float32 [8192, 512], P('fsdp')
- new_momentum: float32 [8192, 512], P('fsdp')
All inputs are finite; a program needn't handle non-finite values.
Results may differ from a plain program's by a relative error of at most 0.0065.
Values may be sent and summed in bfloat16 or wider, within the bound.
A program may use at most 128 MiB of HBM per device.

v0:
```python
import math

import jax
import jax.numpy as jnp
from jax import lax
from jax.sharding import PartitionSpec as P

HD = 128
KV_HEADS = 4


def rope_tables(positions, size):
    half = size // 2
    steps = jnp.arange(half).astype(jnp.float32)
    freqs = jnp.exp(steps * (-2.0 * math.log(500000.0) / size))
    angle = positions.astype(jnp.float32)[:, None] * freqs[None, :]
    return (jnp.cos(angle)[:, None, :], jnp.sin(angle)[:, None, :])


def rotate_keys(plain, cosine, sine, heads, size):
    count = plain.shape[0]
    half = size // 2
    shaped = plain.reshape(count, heads, size)
    first = shaped[:, :, :half]
    second = shaped[:, :, half:]
    out = jnp.concatenate([first * cosine - second * sine, second * cosine + first * sine], axis=2)
    return out.reshape(count, heads * size)


def unrotate_grad(upper, cosine, sine, heads, size):
    count = upper.shape[0]
    half = size // 2
    shaped = upper.astype(jnp.float32).reshape(count, heads, size)
    first = shaped[:, :, :half]
    second = shaped[:, :, half:]
    out = jnp.concatenate([first * cosine + second * sine, second * cosine - first * sine], axis=2)
    return out.reshape(count, heads * size)


def outer_update(delta_sum, count, anchor_rows, momentum_rows):
    mean_delta = delta_sum / count
    momentum_next = 0.9 * momentum_rows + mean_delta
    anchor_next = anchor_rows - 0.7 * (mean_delta + 0.9 * momentum_next)
    return (anchor_next, momentum_next)


def local(
    embedded,
    positions,
    key_cotangent,
    local_weight,
    adam_first,
    adam_second,
    pseudo_grad,
    anchor,
    momentum,
):
    inputs = embedded[0]
    weight = local_weight[0]
    weight_b = weight.astype(jnp.bfloat16)
    columns = inputs
    plain = jnp.dot(
        columns,
        lax.all_gather(weight_b, "fsdp", axis=0, tiled=True),
        preferred_element_type=jnp.float32,
    )
    cosine, sine = rope_tables(positions[0], HD)
    keys = rotate_keys(plain, cosine, sine, KV_HEADS, HD).astype(jnp.bfloat16)
    key_grad = unrotate_grad(key_cotangent[0], cosine, sine, KV_HEADS, HD).astype(jnp.bfloat16)
    columns = inputs
    grad = lax.psum_scatter(
        lax.dot_general(
            columns, key_grad, (((0,), (0,)), ((), ())), preferred_element_type=jnp.float32
        ).astype(jnp.bfloat16),
        "fsdp",
        scatter_dimension=0,
        tiled=True,
    ).astype(jnp.float32)
    first = 0.9 * adam_first[0] + 0.1 * grad
    second = 0.999 * adam_second[0] + 0.001 * grad * grad
    stepped = weight - 0.001 * (first / (jnp.sqrt(second) + 1e-08) + 0.1 * weight)
    replicas = lax.axis_size("replica")
    delta_sum = lax.psum(pseudo_grad[0].astype(jnp.bfloat16), "replica").astype(jnp.float32)
    anchor_next, momentum_next = outer_update(delta_sum, replicas, anchor, momentum)
    merged = 0.5 * anchor_next + 0.5 * stepped
    return (keys[None], merged[None], first[None], second[None], anchor_next, momentum_next)


def solution(mesh):
    return jax.shard_map(
        local,
        mesh=mesh,
        in_specs=(
            P("replica", "fsdp", None),
            P("replica", "fsdp"),
            P("replica", "fsdp", None),
            P("replica", "fsdp", None),
            P("replica", "fsdp", None),
            P("replica", "fsdp", None),
            P("replica", "fsdp", None),
            P("fsdp", None),
            P("fsdp", None),
        ),
        out_specs=(
            P("replica", "fsdp", None),
            P("replica", "fsdp", None),
            P("replica", "fsdp", None),
            P("replica", "fsdp", None),
            P("fsdp", None),
            P("fsdp", None),
        ),
        check_vma=False,
    )
```

profile of v0, /device:TPU:1, one launch (start us, length us, event | category | flops | bytes accessed | tf_op | source)
XLA Modules:
  0.0 310.8 jit_solution(18365839100280375367)
XLA Ops:
  8.0 0.0 all-gather.2.cloned.1.call-start
  8.0 1.2 copy.15
  9.3 0.7 bitcast_convert_fusion
  10.0 0.0 all-gather.2.cloned.1.call-update
  10.0 0.0 all-reduce.2.cloned.1.call-start
  10.1 1.9 copy.16
  12.0 0.0 all-reduce.2.cloned.1.call-update
  12.0 0.0 reduce-scatter.2.cloned.1.call-start
  12.1 0.7 convert_reduce_fusion
  12.8 1.2 copy.20
  13.9 0.4 multiply_cosine_fusion
  14.4 112.8 %all-gather.2.cloned.1.call-done = bf16[8192,512]{0,1:T(8,128)(2,1)} async-done(((bf16[256,512]{0,1:T(8,128)(2,1)}), bf16[8192,512]{0,1:T(8,128)(2,1)}) %all-gather.2.cloned.1.call-update) | async-done | bytes 8388624 | tf_op jit(solution)/shard_map/all_gather | solution.py:64
  127.2 8.8 %fusion.1 = f32[384,4,128]{0,2,1:T(8,128)S(1)} fusion(bf16[4,128,8192]{2,1,0:T(8,128)(2,1)} %bitcast.57, bf16[1,384,8192]{2,1,0:T(8,128)(2,1)} %param.9), kind=kOutput, calls=%fused_computation.2 | convolution fusion | flops 3221225472 | bytes 15466496 | tf_op jit(solution)/shard_map/dot_general | solution.py:62
  136.0 0.2 add_convert_fusion
  136.2 0.1 pad_maximum_fusion
  136.3 0.0 copy-start
  136.3 9.5 %fusion = bf16[8192,512]{0,1:T(8,128)(2,1)} fusion(bf16[384,512]{0,1:T(8,128)(2,1)S(1)} %bitcast.56, bf16[1,384,8192]{2,1,0:T(8,128)(2,1)} %param.9), kind=kOutput, calls=%fused_computation.1 | convolution fusion | flops 3225419776 | bytes 15073280 | tf_op jit(solution)/shard_map/dot_general | solution.py:72
  145.9 0.0 reduce-scatter.2.cloned.1.call-update
  145.9 0.0 copy-done
  145.9 0.2 copy.17
  146.1 0.8 copy-done.1
  146.9 0.2 copy.18
  147.1 0.2 copy.19
  147.3 1.2 copy.21
  148.6 0.9 copy.22
  149.5 141.8 %reduce-scatter.2.cloned.1.call-done = bf16[256,512]{0,1:T(8,128)(2,1)} async-done(((bf16[8192,512]{0,1:T(8,128)(2,1)}), bf16[256,512]{0,1:T(8,128)(2,1)}) %reduce-scatter.2.cloned.1.call-update) | async-done | bytes 262160 | tf_op jit(solution)/shard_map/reduce_scatter | solution.py:71
  291.3 2.9 fusion.10
  294.2 2.0 copy.23
  296.2 2.0 copy.24
  298.3 2.0 copy.25
  300.3 2.0 copy.26
  302.3 1.0 copy.27
  (5 shorter events, 0.0 us)
Async XLA Ops:
  8.0 119.2 %all-gather.2.cloned.1.call-start = ((), (), s32[]{:S(2)}) async-start(), calls=%async_computation.1 | async-start | bytes 8650752 | tf_op jit(solution)/shard_map/all_gather | solution.py:64
  10.0 139.5 %all-reduce.2.cloned.1.call-start = ((), (), s32[]{:S(2)}) async-start(), calls=%async_computation.2 | async-start | bytes 524288 | tf_op jit(solution)/shard_map/psum | solution.py:83
  12.0 279.3 %reduce-scatter.2.cloned.1.call-start = ((), (), s32[]{:S(2)}) async-start(), calls=%async_computation.3 | async-start | bytes 8650752 | tf_op jit(solution)/shard_map/reduce_scatter | solution.py:71
  136.3 9.6 %copy-start = (f32[256,512]{1,0:T(8,128)S(1)}, f32[256,512]{1,0:T(8,128)}, u32[]{:S(2)}) copy-start(f32[256,512]{1,0:T(8,128)} %param.17) | copy-start | bytes 1572868
  145.9 1.0 copy-start.1
  145.9 1.2 copy-start.2
Sparse Core Ops, SparseCore 0:
  12.0 115.1 all-gather.1
  146.0 145.2 reduce-scatter.1
Sparse Core Ops, SparseCore 1:
  13.7 78.1 all-reduce.1
where the time goes:
time: 315 us; the launch traced here: 311 us
  waiting for transfers between devices  255 us (81%)
  matrix products  18.3 us (6%)
  local copies, waits for them, and re-layouts  17 us (5%)
  between operations  15.6 us (5%)
  other arithmetic  5.04 us (2%)
    reduce_scatter x1, waiting for transfers between devices, local(): lax.psum_scatter(lax.dot_general(columns, key_grad, (((0,), (0,)), ((), (...  142 us
    all_gather x1, waiting for transfers between devices, local(): lax.all_gather(weight_b, 'fsdp', axis=0, tiled=True)  113 us
    unnamed x18, local copies, waits for them, and re-layouts  15.8 us
    dot_general x1, matrix products, local(): lax.dot_general(columns, key_grad, (((0,), (0,)), ((), ())), preferred_el...  9.55 us
    dot_general x1, matrix products, local(): jnp.dot(columns, lax.all_gather(weight_b, 'fsdp', axis=0, tiled=True), pr...  8.79 us
  transfers between devices with their start and end apart: 3, of which 2 were waited for; matrix products, arithmetic and copies ran while one was open for 8% of the time, Pallas kernels for 0%

commit v1 on v0

v1 whole, which is shorter than its diff:
```python
import functools
import math

import jax
import jax.numpy as jnp
import numpy as np
from jax import lax
from jax.experimental import pallas as pl
from jax.experimental.pallas import tpu as pltpu
from jax.sharding import PartitionSpec as P

HD = 128
KV_HEADS = 4
NZ = 8
NX = 4
TOK = 384
ROWS = 256
KW = 512
HALF = 256
MESH = pl.DeviceIdType.MESH
F32 = jnp.float32
BF16 = jnp.bfloat16


def frequencies():
    steps = np.arange(HD // 2, dtype=np.float64)
    freqs = np.exp(steps * (-2.0 * math.log(500000.0) / HD)).astype(np.float32)
    return np.concatenate([freqs, freqs])[None, :]


def kernel(
    emb, pos, freq, cot, weight, pseudo,
    keys_out, grad_out, delta_out,
    emba, wall, wf, cotv, psv, psb, kgt, ysend, yrecv, own, zs, zr, acc, accx,
    cosv, sinv, keyv, gout, p1, p2s, p2r, dsum,
    loc, embl, embs, embr, kgs, kgr, ags, agr, yas, yar, yss, yrr, zss, zrr, xs, xr, p1ss, p1rr, p2ss, p2rr, p3ss, p3rr, outs,
):
    r = lax.axis_index("replica")
    f = lax.axis_index("fsdp")
    ylo, x = r // NX, r % NX
    z, yh, c = f // 4, (f // 2) % 2, f % 2

    def wrap(v):
        return lax.rem(v + 2 * NZ, NZ)

    def at_z(v):
        return (r, wrap(v) * 4 + yh * 2 + c)

    nexts = (at_z(z + 1), at_z(z - 1))
    across = (r, z * 4 + (1 - yh) * 2 + c)
    twin = (r, z * 4 + yh * 2 + (1 - c))
    xpeers = [(ylo * NX + lax.rem(x + k, NX), f) for k in (1, 2, 3)]
    ypeer = ((1 - ylo) * NX + x, f)

    def remote(src, dst, ss, rs, dev):
        return pltpu.make_async_remote_copy(
            src_ref=src, dst_ref=dst, send_sem=ss, recv_sem=rs, device_id=dev, device_id_type=MESH
        )

    def slot(zz, plane):
        return wrap(zz) * 2 + plane

    def place(j):
        i = j % 8
        away = (4 - (i + 1) // 2) * (2 * (i % 2) - 1)
        return slot(z + away, jnp.where(j < 8, 1 - yh, yh))

    load_w = pltpu.make_async_copy(weight, wf, loc.at[0])
    load_c = pltpu.make_async_copy(cot, cotv, loc.at[1])
    load_p = pltpu.make_async_copy(pseudo, psv, loc.at[2])

    def load_emb(j):
        b = place(j)
        cols = pl.multiple_of((2 * b + c) * ROWS, ROWS)
        return pltpu.make_async_copy(emb.at[:, pl.ds(cols, ROWS)], emba.at[b, pl.ds(0, TOK)], embl.at[j])

    def swap_emb(j):
        b = place(j)
        cols = pl.multiple_of((2 * b + 1 - c) * ROWS, ROWS)
        return remote(
            emb.at[:, pl.ds(cols, ROWS)], emba.at[b, pl.ds(TOK, TOK)], embs.at[j], embr.at[j], twin
        )

    load_w.start()
    load_c.start()
    load_p.start()
    lax.fori_loop(0, 16, lambda j, _: (load_emb(j).start(), 0)[1], 0)

    barrier = pltpu.get_barrier_semaphore()
    friends = [*nexts, across, twin, *xpeers, ypeer]
    for dev in friends:
        pl.semaphore_signal(barrier, inc=1, device_id=dev, device_id_type=MESH)

    load_w.wait()
    mine = slot(z, yh)
    other = slot(z, 1 - yh)
    wall[mine] = wf[...].astype(BF16)
    pl.semaphore_wait(barrier, len(friends))

    def ring(way, k):
        d, p = k // 2, k % 2
        sign = 1 if way == 0 else -1
        b = slot(z - sign * d, yh if p == 0 else 1 - yh)
        if d < 3:
            ref = wall.at[b]
        else:
            ref = wall.at[b, pl.ds(way * (ROWS // 2), ROWS // 2)]
        return remote(ref, ref, ags.at[way, k], agr.at[way, k], nexts[way])

    def ring_in(way, k):
        d, p = k // 2, k % 2
        sign = 1 if way == 0 else -1
        b = slot(z - sign * (d + 1), yh if p == 0 else 1 - yh)
        if d < 3:
            ref = wall.at[b]
        else:
            ref = wall.at[b, pl.ds(way * (ROWS // 2), ROWS // 2)]
        return remote(ref, ref, ags.at[way, k], agr.at[way, k], nexts[way])

    ring(0, 0).start()
    ring(1, 0).start()
    cross = remote(wall.at[mine], wall.at[mine], yas.at[0], yar.at[0], across)
    cross_in = remote(wall.at[other], wall.at[other], yas.at[0], yar.at[0], across)
    cross.start()
    lax.fori_loop(0, 16, lambda j, _: (swap_emb(j).start(), 0)[1], 0)

    posf = pos[...].astype(F32)
    cols = [
        jnp.transpose(jnp.broadcast_to(posf[:, 128 * j : 128 * (j + 1)], (128, 128))) for j in range(3)
    ]
    lane = lax.broadcasted_iota(jnp.int32, (192, 128), 1)
    low = lane < HD // 2
    lower = jnp.concatenate([cols[0], cols[1][:64]], axis=0)
    upper = jnp.concatenate([cols[1][64:], cols[2]], axis=0)
    angle = jnp.where(low, lower, upper) * freq[...]
    cp, sp = jnp.cos(angle), jnp.sin(angle)
    cq, sq = pltpu.roll(cp, 64, 1), pltpu.roll(sp, 64, 1)
    cosv[0:192, :] = jnp.where(low, cp, cq)
    cosv[192:384, :] = jnp.where(low, cq, cp)
    sinv[0:192, :] = jnp.where(low, -sp, sq)
    sinv[192:384, :] = jnp.where(low, -sq, sp)

    load_c.wait()
    for h in range(KV_HEADS):
        u = cotv[:, h * HD : (h + 1) * HD].astype(F32)
        g = u * cosv[...] - pltpu.roll(u, 64, 1) * sinv[...]
        kgt[h * HD : (h + 1) * HD, 0:TOK] = jnp.transpose(g).astype(BF16)
    give_kg = remote(kgt.at[:, pl.ds(0, TOK)], kgt.at[:, pl.ds(TOK, TOK)], kgs.at[0], kgr.at[0], twin)
    give_kg.start()

    load_p.wait()
    psb[...] = psv[...].astype(BF16)

    def piece(xx):
        return pl.ds(pl.multiple_of(xx * 64, 64), 64)

    stage1 = [
        remote(psb.at[piece(lax.rem(x + k, NX))], p1.at[k - 1], p1ss.at[k - 1], p1rr.at[k - 1], xpeers[k - 1])
        for k in (1, 2, 3)
    ]
    for cp1 in stage1:
        cp1.start()

    def block(j):
        load_emb(j).wait()
        swap_emb(j).wait_recv()
        return jnp.dot(kgt[...], emba[place(j)], preferred_element_type=F32)

    def send_y(i):
        return remote(ysend.at[i], yrecv.at[i], yss.at[i], yrr.at[i], across)

    def far(i, send):
        ysend[i] = block(i).astype(BF16)
        if send:
            send_y(i).start()
        return 0

    def near(i, _):
        own[i] = block(i + 8)
        return 0

    give_kg.wait_recv()
    lax.fori_loop(0, 3, lambda i, _: far(i, True), 0)

    cross_in.wait_recv()
    ring(0, 1).start()
    ring(1, 1).start()

    lax.fori_loop(3, 8, lambda i, _: far(i, False), 0)

    def advance(k):
        for way in (0, 1):
            ring_in(way, k).wait_recv()
            if k + 2 < 8:
                ring(way, k + 2).start()

    advance(0)
    lax.fori_loop(0, 8, near, 0)

    def product(b, first=False):
        def part(m, _):
            at = pl.ds(pl.multiple_of(m * 256, 256), 256)
            value = jnp.dot(emba[b, at, :], wall[b], preferred_element_type=F32)
            if first:
                acc[at, :] = value
            else:
                acc[at, :] += value
            return 0

        lax.fori_loop(0, 3, part, 0)

    def products(k):
        d, p = k // 2, k % 2
        plane = yh if p == 0 else 1 - yh
        product(slot(z - d - 1, plane))
        if d < 3:
            product(slot(z + d + 1, plane))

    product(mine, True)
    product(other)

    for cp1 in stage1:
        cp1.wait_recv()
    part_sum = psb[piece(x), :].astype(F32)
    for k in range(3):
        part_sum = part_sum + p1[k].astype(F32)
    p2s[...] = part_sum.astype(BF16)
    stage2 = remote(p2s, p2r, p2ss.at[0], p2rr.at[0], ypeer)
    stage2.start()

    def next_y(i):
        send_y(i - 3).wait_send()
        send_y(i).start()

    def hand(way, step, h):
        rows = pl.ds(h * HALF, HALF)
        return remote(
            zs.at[way, step, rows], zr.at[way, step, rows],
            zss.at[way, step * 2 + h], zrr.at[way, step * 2 + h], nexts[way],
        )

    def here(i, h):
        rows = pl.ds(h * HALF, HALF)
        return own[i, rows, :] + yrecv[i, rows, :].astype(F32)

    def relay(i, way, step):
        send_y(i).wait_recv()
        halves = (1, 0) if way == 0 else (0, 1)
        for h in halves:
            rows = pl.ds(h * HALF, HALF)
            total = here(i, h)
            if step > 1 or h == way:
                hand(way, step - 1, h).wait_recv()
                total = total + zr[way, step - 1, rows, :].astype(F32)
            zs[way, step, rows, :] = total.astype(BF16)
            hand(way, step, h).start()

    next_y(3)
    send_y(0).wait_recv()
    for way in (0, 1):
        rows = pl.ds(way * HALF, HALF)
        zs[way, 0, rows, :] = here(0, way).astype(BF16)
        hand(way, 0, way).start()
    advance(1)
    products(0)
    products(1)
    next_y(4)
    relay(1, 0, 1)

    stage2.wait_recv()
    dsum[piece(x), :] = (p2s[...].astype(F32) + p2r[...].astype(F32)).astype(BF16)
    stage3 = [
        remote(dsum.at[piece(x)], dsum.at[piece(x)], p3ss.at[k - 1], p3rr.at[k - 1], xpeers[k - 1])
        for k in (1, 2, 3)
    ]
    stage3_in = [
        remote(
            dsum.at[piece(lax.rem(x + NX - k, NX))], dsum.at[piece(lax.rem(x + NX - k, NX))],
            p3ss.at[k - 1], p3rr.at[k - 1], xpeers[k - 1],
        )
        for k in (1, 2, 3)
    ]
    for cp3 in stage3:
        cp3.start()

    advance(2)
    products(2)
    next_y(5)
    relay(2, 1, 1)
    advance(3)
    products(3)
    next_y(6)
    relay(3, 0, 2)
    for cp3 in stage3_in:
        cp3.wait_recv()
    save_d = pltpu.make_async_copy(dsum, delta_out, outs.at[0])
    save_d.start()
    advance(4)
    products(4)
    next_y(7)
    relay(4, 1, 2)
    advance(5)
    products(5)
    relay(5, 0, 3)
    advance(6)
    products(6)
    relay(6, 1, 3)
    advance(7)
    products(7)

    give_x = remote(acc.at[pl.ds(TOK, TOK)], accx, xs.at[0], xr.at[0], twin)
    give_x.start()
    give_x.wait_recv()
    for h in range(KV_HEADS):
        at = slice(h * HD, (h + 1) * HD)
        plain = acc[0:TOK, at] + accx[:, at]
        keyv[:, at] = (plain * cosv[...] + pltpu.roll(plain, 64, 1) * sinv[...]).astype(BF16)
    save_k = pltpu.make_async_copy(keyv, keys_out, outs.at[1])
    save_k.start()

    send_y(7).wait_recv()
    for h in (0, 1):
        rows = pl.ds(h * HALF, HALF)
        total = here(7, h)
        for way in (0, 1):
            hand(way, 3, h).wait_recv()
            total = total + zr[way, 3, rows, :].astype(F32)
        gout[:, h * HALF : (h + 1) * HALF] = jnp.transpose(total)
    save_g = pltpu.make_async_copy(gout, grad_out, outs.at[2])
    save_g.start()

    for k in range(8):
        for way in (0, 1):
            ring(way, k).wait_send()
    cross.wait_send()
    lax.fori_loop(0, 16, lambda j, _: (swap_emb(j).wait_send(), 0)[1], 0)
    give_kg.wait_send()
    give_x.wait_send()
    for i in (5, 6, 7):
        send_y(i).wait_send()
    for way in (0, 1):
        for step in range(4):
            for h in (0, 1):
                if step > 0 or h == way:
                    hand(way, step, h).wait_send()
    for cp in [*stage1, stage2, *stage3]:
        cp.wait_send()
    save_d.wait()
    save_k.wait()
    save_g.wait()


def step(embedded, positions, cotangent, weight, pseudo):
    any_spec = pl.BlockSpec(memory_space=pl.ANY)
    vmem_spec = pl.BlockSpec(memory_space=pltpu.VMEM)
    dma = pltpu.SemaphoreType.DMA
    return pl.pallas_call(
        kernel,
        out_shape=(
            jax.ShapeDtypeStruct((TOK, KW), BF16),
            jax.ShapeDtypeStruct((ROWS, KW), F32),
            jax.ShapeDtypeStruct((ROWS, KW), BF16),
        ),
        in_specs=[any_spec, vmem_spec, vmem_spec, any_spec, any_spec, any_spec],
        out_specs=(any_spec, any_spec, any_spec),
        scratch_shapes=[
            pltpu.VMEM((16, 2 * TOK, ROWS), BF16),
            pltpu.VMEM((16, ROWS, KW), BF16),
            pltpu.VMEM((ROWS, KW), F32),
            pltpu.VMEM((TOK, KW), BF16),
            pltpu.VMEM((ROWS, KW), F32),
            pltpu.VMEM((ROWS, KW), BF16),
            pltpu.VMEM((KW, 2 * TOK), BF16),
            pltpu.VMEM((8, KW, ROWS), BF16),
            pltpu.VMEM((8, KW, ROWS), BF16),
            pltpu.VMEM((8, KW, ROWS), F32),
            pltpu.VMEM((2, 4, KW, ROWS), BF16),
            pltpu.VMEM((2, 4, KW, ROWS), BF16),
            pltpu.VMEM((2 * TOK, KW), F32),
            pltpu.VMEM((TOK, KW), F32),
            pltpu.VMEM((TOK, HD), F32),
            pltpu.VMEM((TOK, HD), F32),
            pltpu.VMEM((TOK, KW), BF16),
            pltpu.VMEM((ROWS, KW), F32),
            pltpu.VMEM((3, 64, KW), BF16),
            pltpu.VMEM((64, KW), BF16),
            pltpu.VMEM((64, KW), BF16),
            pltpu.VMEM((ROWS, KW), BF16),
            dma((3,)),
            dma((16,)),
            dma((16,)),
            dma((16,)),
            dma((1,)),
            dma((1,)),
            dma((2, 8)),
            dma((2, 8)),
            dma((1,)),
            dma((1,)),
            dma((8,)),
            dma((8,)),
            dma((2, 8)),
            dma((2, 8)),
            dma((1,)),
            dma((1,)),
            dma((3,)),
            dma((3,)),
            dma((1,)),
            dma((1,)),
            dma((3,)),
            dma((3,)),
            dma((3,)),
        ],
        compiler_params=pltpu.CompilerParams(
            collective_id=0, has_side_effects=True, vmem_limit_bytes=48 * 1024 * 1024
        ),
        cost_estimate=pl.CostEstimate(flops=6442450944, bytes_accessed=10 << 20, transcendentals=0),
    )(embedded, positions, jnp.asarray(frequencies()), cotangent, weight, pseudo)


def outer_update(delta_sum, count, anchor_rows, momentum_rows):
    mean_delta = delta_sum / count
    momentum_next = 0.9 * momentum_rows + mean_delta
    anchor_next = anchor_rows - 0.7 * (mean_delta + 0.9 * momentum_next)
    return (anchor_next, momentum_next)


def local(
    embedded,
    positions,
    key_cotangent,
    local_weight,
    adam_first,
    adam_second,
    pseudo_grad,
    anchor,
    momentum,
):
    weight = local_weight[0]
    keys, grad, delta = step(embedded[0], positions, key_cotangent[0], weight, pseudo_grad[0])
    first = 0.9 * adam_first[0] + 0.1 * grad
    second = 0.999 * adam_second[0] + 0.001 * grad * grad
    stepped = weight - 0.001 * (first / (jnp.sqrt(second) + 1e-08) + 0.1 * weight)
    replicas = lax.axis_size("replica")
    anchor_next, momentum_next = outer_update(delta.astype(F32), replicas, anchor, momentum)
    merged = 0.5 * anchor_next + 0.5 * stepped
    return (keys[None], merged[None], first[None], second[None], anchor_next, momentum_next)


def solution(mesh):
    return jax.shard_map(
        local,
        mesh=mesh,
        in_specs=(
            P("replica", "fsdp", None),
            P("replica", "fsdp"),
            P("replica", "fsdp", None),
            P("replica", "fsdp", None),
            P("replica", "fsdp", None),
            P("replica", "fsdp", None),
            P("replica", "fsdp", None),
            P("fsdp", None),
            P("fsdp", None),
        ),
        out_specs=(
            P("replica", "fsdp", None),
            P("replica", "fsdp", None),
            P("replica", "fsdp", None),
            P("replica", "fsdp", None),
            P("fsdp", None),
            P("fsdp", None),
        ),
        check_vma=False,
    )
```

time: 315 us -> 83.6 us (0.27); the launches traced: 311 us -> 83.3 us
  waiting for transfers between devices: 255 us -> 0 us
  Pallas kernels: 0 us -> 75.8 us
  matrix products: 18.3 us -> 0 us
  between operations: 15.6 us -> 0.69 us
  local copies, waits for them, and re-layouts: 17 us -> 5.17 us
  other arithmetic: 5.04 us -> 1.67 us
    reduce_scatter x1 -> x0, waiting for transfers between devices: 142 us -> none  [local(): lax.psum_scatter(lax.dot_general(columns, key_grad, (((0,), (0,)), ((), (...]
    all_gather x1 -> x0, waiting for transfers between devices: 113 us -> none  [local(): lax.all_gather(weight_b, 'fsdp', axis=0, tiled=True)]
    pallas_call x0 -> x1, Pallas kernels: none -> 75.8 us  [step(): pl.pallas_call(kernel, out_shape=(jax.ShapeDtypeStruct((TOK, KW), BF16),...]
    dot_general x2 -> x0, matrix products: 18.3 us -> none  [the longest x1 9.55 us: local(): lax.dot_general(columns, key_grad, (((0,), (0,)), ((), ())), preferred_el...]
    unnamed x18 -> x19, local copies, waits for them, and re-layouts: 15.8 us -> 5.17 us
  transfers between devices with their start and end apart: 3 -> 0, of which waited for: 2 -> 0; matrix products, arithmetic and copies ran while one was open for 8% -> 0% of each run, Pallas kernels for 0% -> 0%
where the time goes in v1:
time: 83.6 us; the launch traced here: 83.3 us
  Pallas kernels  75.8 us (91%)
  local copies, waits for them, and re-layouts  5.17 us (6%)
  other arithmetic  1.67 us (2%)
    pallas_call x1, Pallas kernels, step(): pl.pallas_call(kernel, out_shape=(jax.ShapeDtypeStruct((TOK, KW), BF16),...  75.8 us
    unnamed x19, local copies, waits for them, and re-layouts  5.17 us

profile of v1, /device:TPU:1, one launch (start us, length us, event | category | flops | bytes accessed | tf_op | source)
XLA Modules:
  0.0 83.3 jit_solution(18107606319794239144)
XLA Ops:
  0.6 0.0 copy-start
  0.6 1.0 %copy-done = f32[1,256,512]{2,1,0:T(8,128)S(1)} copy-done((f32[1,256,512]{2,1,0:T(8,128)S(1)}, f32[1,256,512]{2,1,0:T(8,128)}, u32[]{:S(2)}) %copy-start) | copy-done | bytes 524312
  1.7 0.0 copy-start.1
  1.7 1.0 %copy-done.1 = f32[1,256,512]{2,1,0:T(8,128)S(1)} copy-done((f32[1,256,512]{2,1,0:T(8,128)S(1)}, f32[1,256,512]{2,1,0:T(8,128)}, u32[]{:S(2)}) %copy-start.1) | copy-done | bytes 524312
  2.7 0.0 copy-start.2
  2.7 1.0 %copy-done.2 = bf16[1,384,512]{2,1,0:T(8,128)(2,1)S(1)} copy-done((bf16[1,384,512]{2,1,0:T(8,128)(2,1)S(1)}, bf16[1,384,512]{2,1,0:T(8,128)(2,1)}, u32[]{:S(2)}) %copy-start.2) | copy-done | bytes 393240
  3.7 0.0 copy-start.3
  3.7 0.7 copy-done.3
  4.4 0.0 copy-start.4
  4.4 0.7 copy-done.4
  5.1 0.0 copy-start.5
  5.1 0.0 copy-start.6
  5.1 0.0 copy-start.7
  5.1 0.0 copy-start.8
  5.1 75.8 %shard_map.145 = (bf16[384,512]{1,0:T(8,128)(2,1)S(1)}, f32[256,512]{1,0:T(8,128)S(1)}, bf16[256,512]{1,0:T(8,128)(2,1)S(1)}) custom-call(bf16[384,8192]{1,0:T(8,128)(2,1)} %bitcast.28, s32[1,384]{1,0:T(1,128)S(1)} %copy-done.3, f32[1,128]{1,0:T(1,128)S(1)} %copy-done.4, bf16[384,512]{1,0:T(8,128)(2,1)S(1)} %bitcast.27, f32[256,512]{1,0:T(8,128)S(1)} %bitcast.24, ...), custom_call_target="tpu_custom_call" | custom-call | flops 6442450944 | bytes 10485760 | tf_op jit(solution)/shard_map/pallas_call | solution.py:357
  80.9 0.0 copy-done.5
  80.9 0.0 copy-done.6
  80.9 0.0 copy-done.7
  80.9 0.0 copy-done.8
  80.9 1.7 %multiply_bitcast_fusion = (f32[1,256,512]{2,1,0:T(8,128)}, f32[256,512]{1,0:T(8,128)}, f32[256,512]{1,0:T(8,128)}, f32[1,256,512]{2,1,0:T(8,128)}, f32[1,256,512]{2,1,0:T(8,128)}) fusion(f32[256,512]{1,0:T(8,128)S(1)} %get-tuple-element.11, f32[1,256,512]{2,1,0:T(8,128)S(1)} %copy-done.5, f32[1,256,512]{2,1,0:T(8,128)S(1)} %copy-done.6, ...), kind=kLoop, calls=%fused_computation.3 | loop fusion | flops 3014656 | bytes 6029312 | tf_op jit(solution)/shard_map/broadcast_in_dim | solution.py:446
  82.6 0.7 copy.17
Async XLA Ops:
  0.6 1.0 %copy-start = (f32[1,256,512]{2,1,0:T(8,128)S(1)}, f32[1,256,512]{2,1,0:T(8,128)}, u32[]{:S(2)}) copy-start(f32[1,256,512]{2,1,0:T(8,128)} %param.13) | copy-start | bytes 1572868
  1.7 1.0 %copy-start.1 = (f32[1,256,512]{2,1,0:T(8,128)S(1)}, f32[1,256,512]{2,1,0:T(8,128)}, u32[]{:S(2)}) copy-start(f32[1,256,512]{2,1,0:T(8,128)} %param.16) | copy-start | bytes 1572868
  2.7 1.0 %copy-start.2 = (bf16[1,384,512]{2,1,0:T(8,128)(2,1)S(1)}, bf16[1,384,512]{2,1,0:T(8,128)(2,1)}, u32[]{:S(2)}) copy-start(bf16[1,384,512]{2,1,0:T(8,128)(2,1)} %param.12) | copy-start | bytes 1179652
  3.7 0.7 copy-start.3
  4.4 0.7 copy-start.4
  5.1 75.8 %copy-start.5 = (f32[1,256,512]{2,1,0:T(8,128)S(1)}, f32[1,256,512]{2,1,0:T(8,128)}, u32[]{:S(2)}) copy-start(f32[1,256,512]{2,1,0:T(8,128)} %param.14) | copy-start | bytes 1572868
  5.1 75.8 %copy-start.6 = (f32[1,256,512]{2,1,0:T(8,128)S(1)}, f32[1,256,512]{2,1,0:T(8,128)}, u32[]{:S(2)}) copy-start(f32[1,256,512]{2,1,0:T(8,128)} %param.15) | copy-start | bytes 1572868
  5.1 75.8 %copy-start.7 = (f32[256,512]{1,0:T(8,128)S(1)}, f32[256,512]{1,0:T(8,128)}, u32[]{:S(2)}) copy-start(f32[256,512]{1,0:T(8,128)} %param.17) | copy-start | bytes 1572868
  5.1 75.8 %copy-start.8 = (f32[256,512]{1,0:T(8,128)S(1)}, f32[256,512]{1,0:T(8,128)}, u32[]{:S(2)}) copy-start(f32[256,512]{1,0:T(8,128)} %param.18) | copy-start | bytes 1572868

commit v2 on v1

v2 whole, which is shorter than its diff:
```python
import functools
import math

import jax
import jax.numpy as jnp
import numpy as np
from jax import lax
from jax.experimental import pallas as pl
from jax.experimental.pallas import tpu as pltpu
from jax.sharding import PartitionSpec as P

HD = 128
KV_HEADS = 4
NZ = 8
NX = 4
TOK = 384
ROWS = 256
KW = 512
HALF = 256
HOP = 64
AHEAD = 2
MESH = pl.DeviceIdType.MESH
F32 = jnp.float32
BF16 = jnp.bfloat16


def frequencies():
    steps = np.arange(HD // 2, dtype=np.float64)
    freqs = np.exp(steps * (-2.0 * math.log(500000.0) / HD)).astype(np.float32)
    return np.concatenate([freqs, freqs])[None, :]


def kernel(
    emb, pos_in, freq_in, cot, weight, pseudo,
    keyv, gout, dsum,
    emba, wall, wf, cotv, psv, psb, kgt, ysend, yrecv, own, zs, zr, acc, accx,
    cosv, sinv, p1, p2s, p2r, pos, freq,
    loc, embl, embs, embr, kgs, kgr, ags, agr, yas, yar, yss, yrr, zss, zrr, xs, xr, p1ss, p1rr, p2ss, p2rr, p3ss, p3rr,
):
    r = lax.axis_index("replica")
    f = lax.axis_index("fsdp")
    ylo, x = r // NX, r % NX
    z, yh, c = f // 4, (f // 2) % 2, f % 2

    def wrap(v):
        return lax.rem(v + 2 * NZ, NZ)

    def at_z(v):
        return (r, wrap(v) * 4 + yh * 2 + c)

    nexts = (at_z(z + 1), at_z(z - 1))
    across = (r, z * 4 + (1 - yh) * 2 + c)
    twin = (r, z * 4 + yh * 2 + (1 - c))
    xpeers = [(ylo * NX + lax.rem(x + k, NX), f) for k in (1, 2, 3)]
    ypeer = ((1 - ylo) * NX + x, f)

    def remote(src, dst, ss, rs, dev):
        return pltpu.make_async_remote_copy(
            src_ref=src, dst_ref=dst, send_sem=ss, recv_sem=rs, device_id=dev, device_id_type=MESH
        )

    def slot(zz, plane):
        return wrap(zz) * 2 + plane

    def place(j):
        i = j % 8
        away = (4 - (i + 1) // 2) * (2 * (i % 2) - 1)
        return slot(z + away, jnp.where(j < 8, 1 - yh, yh))

    load_w = [
        pltpu.make_async_copy(weight.at[pl.ds(h * 128, 128)], wf.at[pl.ds(h * 128, 128)], loc.at[h]) for h in (0, 1)
    ]
    load_t = pltpu.make_async_copy(pos_in, pos.at[0], loc.at[2])
    load_f = pltpu.make_async_copy(freq_in, freq, loc.at[3])
    load_c = pltpu.make_async_copy(cot, cotv.at[0], loc.at[4])
    load_p = pltpu.make_async_copy(pseudo, psv, loc.at[5])
    load_w[0].start()
    load_w[1].start()
    barrier = pltpu.get_barrier_semaphore()
    friends = [*nexts, across, twin, *xpeers, ypeer]
    for dev in friends:
        pl.semaphore_signal(barrier, inc=1, device_id=dev, device_id_type=MESH)
    load_t.start()
    load_f.start()
    load_c.start()

    mine, other = slot(z, yh), slot(z, 1 - yh)

    def rows_of(k, h):
        if k == 1 and h == 1:
            return pl.ds(128, 128 - HOP)
        return pl.ds(h * 128, 128)

    def travels(way, k, h):
        return h == way if k >= 6 else not (k == 1 and h == 1 and HOP == 128)

    def ring(way, k, h, back=0):
        sign = 1 if way == 0 else -1
        b = slot(z - sign * (k // 2 + back), yh if k % 2 == 0 else 1 - yh)
        ref = wall.at[b, rows_of(k, h)]
        return remote(ref, ref, ags.at[way, k * 2 + h], agr.at[way, k * 2 + h], nexts[way])

    def ring_in(way, k, h):
        return ring(way, k, h, 1)

    def cross(h, b):
        ref = wall.at[b, pl.ds(h * 128, 128)]
        return remote(ref, ref, yas.at[h], yar.at[h], across)

    def hop(way, plane):
        ref = wall.at[slot(z - (1 if way == 0 else -1), plane), pl.ds(ROWS - HOP, HOP)]
        return remote(ref, ref, yas.at[2 + way], yar.at[2 + way], across)

    waited = False
    for h in (0, 1):
        load_w[h].wait()
        wall[mine, h * 128 : (h + 1) * 128, :] = wf[h * 128 : (h + 1) * 128, :].astype(BF16)
        if not waited:
            pl.semaphore_wait(barrier, len(friends))
            waited = True
        ring(0, 0, h).start()
        ring(1, 0, h).start()
        cross(h, mine).start()

    swap_t = remote(pos_in, pos.at[1], kgs.at[0], kgr.at[0], twin)
    swap_c = remote(cot, cotv.at[1], kgs.at[1], kgr.at[1], twin)
    swap_t.start()
    swap_c.start()

    def load_emb(j):
        b = place(j)
        cols = pl.multiple_of((2 * b + c) * ROWS, ROWS)
        return pltpu.make_async_copy(emb.at[:, pl.ds(cols, ROWS)], emba.at[b, pl.ds(0, TOK)], embl.at[j])

    def swap_emb(j):
        b = place(j)
        cols = pl.multiple_of((2 * b + 1 - c) * ROWS, ROWS)
        return remote(emb.at[:, pl.ds(cols, ROWS)], emba.at[b, pl.ds(TOK, TOK)], embs.at[j], embr.at[j], twin)

    def begin(j, _):
        swap_emb(j).start()
        load_emb(j).start()
        return 0

    lax.fori_loop(0, 16, begin, 0)
    load_p.start()

    lane = lax.broadcasted_iota(jnp.int32, (192, 128), 1)
    low = lane < HD // 2

    def tables(t):
        posf = pos[t].astype(F32)
        cols = [jnp.transpose(jnp.broadcast_to(posf[:, 128 * j : 128 * (j + 1)], (128, 128))) for j in range(3)]
        lower = jnp.concatenate([cols[0], cols[1][:64]], axis=0)
        upper = jnp.concatenate([cols[1][64:], cols[2]], axis=0)
        angle = jnp.where(low, lower, upper) * freq[...]
        cp, sp = jnp.cos(angle), jnp.sin(angle)
        cq, sq = pltpu.roll(cp, 64, 1), pltpu.roll(sp, 64, 1)
        cosv[t, 0:192, :] = jnp.where(low, cp, cq)
        cosv[t, 192:384, :] = jnp.where(low, cq, cp)
        sinv[t, 0:192, :] = jnp.where(low, -sp, sq)
        sinv[t, 192:384, :] = jnp.where(low, -sq, sp)
        return 0

    def back(t):
        for h in range(KV_HEADS):
            u = cotv[t, :, h * HD : (h + 1) * HD].astype(F32)
            g = u * cosv[t] - pltpu.roll(u, 64, 1) * sinv[t]
            kgt[h * HD : (h + 1) * HD, t * TOK : (t + 1) * TOK] = jnp.transpose(g).astype(BF16)

    load_t.wait()
    load_f.wait()
    tables(0)
    load_c.wait()
    back(0)
    swap_t.wait_recv()
    tables(1)
    swap_c.wait_recv()
    back(1)

    def block(j):
        load_emb(j).wait()
        swap_emb(j).wait_recv()
        return jnp.dot(kgt[...], emba[place(j)], preferred_element_type=F32)

    def send_y(i, h):
        rows = pl.ds(pl.multiple_of(h * HALF, HALF), HALF)
        return remote(ysend.at[i, rows], yrecv.at[i, rows], yss.at[i, h], yrr.at[i, h], across)

    def far(i, _):
        ysend[i] = block(i).astype(BF16)
        return 0

    def post_y(i):
        send_y(i, i % 2).start()
        send_y(i, 1 - i % 2).start()

    def next_y(i):
        send_y(i - AHEAD, 0).wait_send()
        send_y(i - AHEAD, 1).wait_send()
        post_y(i)

    def near(i, _):
        own[i] = block(i + 8)
        return 0

    def enter(h):
        cross(h, other).wait_recv()
        for way in (0, 1):
            if travels(way, 1, h):
                ring(way, 1, h).start()

    def advance(k, h):
        for way in (0, 1):
            if travels(way, k, h):
                ring_in(way, k, h).wait_recv()
            if k == 1 and h == 1 and HOP:
                hop(way, 1 - yh).wait_recv()
            if k == 0 and h == 1 and HOP:
                hop(way, yh).start()
            if k + 2 < 8 and travels(way, k + 2, h) and (k < 6):
                ring(way, k + 2, h).start()

    far(0, 0)
    post_y(0)
    far(1, 0)
    post_y(1)
    enter(0)
    advance(0, 0)

    load_p.wait()
    psb[...] = psv[...].astype(BF16)

    def piece(xx):
        return pl.ds(pl.multiple_of(xx * 64, 64), 64)

    stage1 = [
        remote(psb.at[piece(lax.rem(x + k, NX))], p1.at[k - 1], p1ss.at[k - 1], p1rr.at[k - 1], xpeers[k - 1])
        for k in (1, 2, 3)
    ]
    for cp1 in stage1:
        cp1.start()

    far(2, 0)
    lax.fori_loop(3, 5, far, 0)
    enter(1)
    advance(0, 1)
    lax.fori_loop(5, 8, far, 0)
    lax.fori_loop(0, 8, near, 0)
    advance(1, 0)

    def product(b, first=False):
        def part(m, _):
            at = pl.ds(pl.multiple_of(m * 256, 256), 256)
            value = jnp.dot(emba[b, at, :], wall[b], preferred_element_type=F32)
            if first:
                acc[at, :] = value
            else:
                acc[at, :] += value
            return 0

        lax.fori_loop(0, 3, part, 0)

    def products(k):
        d, p = k // 2, k % 2
        plane = yh if p == 0 else 1 - yh
        product(slot(z - d - 1, plane))
        if d < 3:
            product(slot(z + d + 1, plane))

    next_y(2)
    product(mine, True)
    product(other)

    for cp1 in stage1:
        cp1.wait_recv()
    part_sum = psb[piece(x), :].astype(F32)
    for k in range(3):
        part_sum = part_sum + p1[k].astype(F32)
    p2s[...] = part_sum.astype(BF16)
    stage2 = remote(p2s, p2r, p2ss.at[0], p2rr.at[0], ypeer)
    stage2.start()

    def hand(way, step, h):
        rows = pl.ds(h * HALF, HALF)
        return remote(
            zs.at[way, step, rows], zr.at[way, step, rows],
            zss.at[way, step * 2 + h], zrr.at[way, step * 2 + h], nexts[way],
        )

    def here(i, h):
        send_y(i, h).wait_recv()
        rows = pl.ds(h * HALF, HALF)
        return own[i, rows, :] + yrecv[i, rows, :].astype(F32)

    def relay(i, way, step, h):
        rows = pl.ds(h * HALF, HALF)
        total = here(i, h)
        if step > 1 or (step == 1 and h == way):
            hand(way, step - 1, h).wait_recv()
            total = total + zr[way, step - 1, rows, :].astype(F32)
        zs[way, step, rows, :] = total.astype(BF16)
        hand(way, step, h).start()

    next_y(3)
    relay(0, 0, 0, 0)
    relay(0, 1, 0, 1)
    products(0)
    advance(1, 1)
    advance(2, 0)
    advance(2, 1)
    products(1)
    next_y(4)
    relay(1, 0, 1, 1)
    relay(1, 0, 1, 0)

    stage2.wait_recv()
    dsum[piece(x), :] = (p2s[...].astype(F32) + p2r[...].astype(F32)).astype(BF16)

    def stage3(k, home):
        ref = dsum.at[piece(home)]
        return remote(ref, ref, p3ss.at[k - 1], p3rr.at[k - 1], xpeers[k - 1])

    for k in (1, 2, 3):
        stage3(k, x).start()

    products(2)
    advance(3, 0)
    advance(3, 1)
    products(3)
    next_y(5)
    relay(2, 1, 1, 0)
    relay(2, 1, 1, 1)
    advance(4, 0)
    advance(4, 1)
    products(4)
    advance(5, 0)
    advance(5, 1)
    products(5)
    next_y(6)
    relay(3, 0, 2, 1)
    relay(3, 0, 2, 0)
    for k in (1, 2, 3):
        stage3(k, lax.rem(x + NX - k, NX)).wait_recv()
    next_y(7)
    relay(4, 1, 2, 0)
    relay(4, 1, 2, 1)
    advance(6, 0)
    advance(6, 1)
    products(6)
    relay(5, 0, 3, 1)
    relay(5, 0, 3, 0)
    advance(7, 0)
    advance(7, 1)
    products(7)

    give_x = remote(acc.at[pl.ds(TOK, TOK)], accx, xs.at[0], xr.at[0], twin)
    give_x.start()
    relay(6, 1, 3, 0)
    relay(6, 1, 3, 1)
    give_x.wait_recv()
    for h in range(KV_HEADS):
        at = slice(h * HD, (h + 1) * HD)
        plain = acc[0:TOK, at] + accx[:, at]
        keyv[:, at] = (plain * cosv[0] + pltpu.roll(plain, 64, 1) * sinv[0]).astype(BF16)

    for h in (0, 1):
        rows = pl.ds(h * HALF, HALF)
        total = here(7, h)
        for way in (0, 1):
            hand(way, 3, h).wait_recv()
            total = total + zr[way, 3, rows, :].astype(F32)
        gout[:, h * HALF : (h + 1) * HALF] = jnp.transpose(total)

    for h in (0, 1):
        cross(h, mine).wait_send()
        for way in (0, 1):
            for k in range(8):
                if travels(way, k, h):
                    ring(way, k, h).wait_send()
    if HOP:
        for way in (0, 1):
            hop(way, yh).wait_send()
    swap_t.wait_send()
    swap_c.wait_send()
    lax.fori_loop(0, 16, lambda j, _: (swap_emb(j).wait_send(), 0)[1], 0)
    give_x.wait_send()

    def sent(i, _):
        send_y(i, 0).wait_send()
        send_y(i, 1).wait_send()
        return 0

    lax.fori_loop(6, 8, sent, 0)
    for way in (0, 1):
        for step in range(4):
            for h in (0, 1):
                if step > 0 or h == way:
                    hand(way, step, h).wait_send()
    for cp1 in stage1:
        cp1.wait_send()
    stage2.wait_send()
    for k in (1, 2, 3):
        stage3(k, x).wait_send()


def step(embedded, positions, cotangent, weight, pseudo):
    vmem_spec = pl.BlockSpec(memory_space=pltpu.VMEM)
    hbm_spec = pl.BlockSpec(memory_space=pltpu.HBM)
    dma = pltpu.SemaphoreType.DMA
    operands = (embedded, positions, jnp.asarray(frequencies()), cotangent, weight, pseudo)
    return pl.pallas_call(
        kernel,
        out_shape=(
            jax.ShapeDtypeStruct((TOK, KW), BF16),
            jax.ShapeDtypeStruct((ROWS, KW), F32),
            jax.ShapeDtypeStruct((ROWS, KW), BF16),
        ),
        in_specs=[hbm_spec] * 6,
        out_specs=(vmem_spec, vmem_spec, vmem_spec),
        scratch_shapes=[
            pltpu.VMEM((16, 2 * TOK, ROWS), BF16),
            pltpu.VMEM((16, ROWS, KW), BF16),
            pltpu.VMEM((ROWS, KW), F32),
            pltpu.VMEM((2, TOK, KW), BF16),
            pltpu.VMEM((ROWS, KW), F32),
            pltpu.VMEM((ROWS, KW), BF16),
            pltpu.VMEM((KW, 2 * TOK), BF16),
            pltpu.VMEM((8, KW, ROWS), BF16),
            pltpu.VMEM((8, KW, ROWS), BF16),
            pltpu.VMEM((8, KW, ROWS), F32),
            pltpu.VMEM((2, 4, KW, ROWS), BF16),
            pltpu.VMEM((2, 4, KW, ROWS), BF16),
            pltpu.VMEM((2 * TOK, KW), F32),
            pltpu.VMEM((TOK, KW), F32),
            pltpu.VMEM((2, TOK, HD), F32),
            pltpu.VMEM((2, TOK, HD), F32),
            pltpu.VMEM((3, 64, KW), BF16),
            pltpu.VMEM((64, KW), BF16),
            pltpu.VMEM((64, KW), BF16),
            pltpu.VMEM((2, 1, TOK), jnp.int32),
            pltpu.VMEM((1, HD), F32),
            dma((6,)),
            dma((16,)),
            dma((16,)),
            dma((16,)),
            dma((2,)),
            dma((2,)),
            dma((2, 16)),
            dma((2, 16)),
            dma((4,)),
            dma((4,)),
            dma((8, 2)),
            dma((8, 2)),
            dma((2, 8)),
            dma((2, 8)),
            dma((1,)),
            dma((1,)),
            dma((3,)),
            dma((3,)),
            dma((1,)),
            dma((1,)),
            dma((3,)),
            dma((3,)),
        ],
        compiler_params=pltpu.CompilerParams(
            collective_id=0, has_side_effects=True, vmem_limit_bytes=48 * 1024 * 1024
        ),
        cost_estimate=pl.CostEstimate(flops=6442450944, bytes_accessed=10 << 20, transcendentals=0),
    )(*(pltpu.with_memory_space_constraint(v, pltpu.HBM) for v in operands))


def outer_update(delta_sum, count, anchor_rows, momentum_rows):
    mean_delta = delta_sum / count
    momentum_next = 0.9 * momentum_rows + mean_delta
    anchor_next = anchor_rows - 0.7 * (mean_delta + 0.9 * momentum_next)
    return (anchor_next, momentum_next)


def local(
    embedded,
    positions,
    key_cotangent,
    local_weight,
    adam_first,
    adam_second,
    pseudo_grad,
    anchor,
    momentum,
):
    weight = local_weight[0]
    keys, grad, delta = step(embedded[0], positions, key_cotangent[0], weight, pseudo_grad[0])
    first = 0.9 * adam_first[0] + 0.1 * grad
    second = 0.999 * adam_second[0] + 0.001 * grad * grad
    stepped = weight - 0.001 * (first / (jnp.sqrt(second) + 1e-08) + 0.1 * weight)
    replicas = lax.axis_size("replica")
    anchor_next, momentum_next = outer_update(delta.astype(F32), replicas, anchor, momentum)
    merged = 0.5 * anchor_next + 0.5 * stepped
    return (keys[None], merged[None], first[None], second[None], anchor_next, momentum_next)


def solution(mesh):
    return jax.shard_map(
        local,
        mesh=mesh,
        in_specs=(
            P("replica", "fsdp", None),
            P("replica", "fsdp"),
            P("replica", "fsdp", None),
            P("replica", "fsdp", None),
            P("replica", "fsdp", None),
            P("replica", "fsdp", None),
            P("replica", "fsdp", None),
            P("fsdp", None),
            P("fsdp", None),
        ),
        out_specs=(
            P("replica", "fsdp", None),
            P("replica", "fsdp", None),
            P("replica", "fsdp", None),
            P("replica", "fsdp", None),
            P("fsdp", None),
            P("fsdp", None),
        ),
        check_vma=False,
    )
```

time: 83.6 us -> 74.5 us (0.89)
  Pallas kernels: 75.8 us -> 71.2 us
  local copies, waits for them, and re-layouts: 5.17 us -> 0.77 us
    pallas_call x1, Pallas kernels: 75.8 us -> 71.2 us  [step(): pl.pallas_call(kernel, out_shape=(jax.ShapeDtypeStruct((TOK, KW), BF16),...]
    unnamed x19 -> x11, local copies, waits for them, and re-layouts: 5.17 us -> 0.77 us
where the time goes in v2:
time: 74.5 us; the launch traced here: 74.4 us
  Pallas kernels  71.2 us (96%)
  other arithmetic  1.69 us (2%)
  local copies, waits for them, and re-layouts  0.77 us (1%)
    pallas_call x1, Pallas kernels, step(): pl.pallas_call(kernel, out_shape=(jax.ShapeDtypeStruct((TOK, KW), BF16),...  71.2 us
    broadcast_in_dim x1, other arithmetic, local(): merged[None]  1.69 us

profile of v2, /device:TPU:1, one launch (start us, length us, event | category | flops | bytes accessed | tf_op | source)
XLA Modules:
  0.0 74.4 jit_solution(7704896963228434338)
XLA Ops:
  0.6 0.0 copy-start
  0.6 0.0 copy-start.1
  0.7 0.0 copy-start.2
  0.7 0.0 copy-start.3
  0.7 0.0 copy-start.4
  0.7 71.2 %shard_map.145 = (bf16[384,512]{1,0:T(8,128)(2,1)S(1)}, f32[256,512]{1,0:T(8,128)S(1)}, bf16[256,512]{1,0:T(8,128)(2,1)S(1)}) custom-call(bf16[384,8192]{1,0:T(8,128)(2,1)} %bitcast.26, s32[1,384]{1,0:T(1,128)} %pos_in.1, f32[1,128]{1,0:T(1,128)} %constant.19.clone.freq_in, bf16[384,512]{1,0:T(8,128)(2,1)} %bitcast.28, f32[256,512]{1,0:T(8,128)} %bitcast.25, ...), custom_call_target="tpu_custom_call" | custom-call | flops 6442450944 | bytes 10485760 | tf_op jit(solution)/shard_map/pallas_call | solution.py:412
  71.9 0.0 copy-done
  71.9 0.0 copy-done.1
  71.9 0.0 copy-done.2
  72.0 0.0 copy-done.3
  72.0 0.0 copy-done.4
  72.0 1.7 %multiply_bitcast_fusion = (f32[1,256,512]{2,1,0:T(8,128)}, f32[256,512]{1,0:T(8,128)}, f32[256,512]{1,0:T(8,128)}, f32[1,256,512]{2,1,0:T(8,128)}, f32[1,256,512]{2,1,0:T(8,128)}) fusion(f32[256,512]{1,0:T(8,128)S(1)} %get-tuple-element.11, f32[1,256,512]{2,1,0:T(8,128)S(1)} %copy-done.1, f32[1,256,512]{2,1,0:T(8,128)S(1)} %copy-done.2, ...), kind=kLoop, calls=%fused_computation.3 | loop fusion | flops 3014656 | bytes 6029312 | tf_op jit(solution)/shard_map/broadcast_in_dim | solution.py:499
  73.7 0.7 %copy.17 = bf16[1,384,512]{2,1,0:T(8,128)(2,1)} copy(bf16[1,384,512]{2,1,0:T(8,128)(2,1)S(1)} %bitcast.24) | data formatting | bytes 786432
Async XLA Ops:
  0.6 71.3 %copy-start = (f32[1,256,512]{2,1,0:T(8,128)S(1)}, f32[1,256,512]{2,1,0:T(8,128)}, u32[]{:S(2)}) copy-start(f32[1,256,512]{2,1,0:T(8,128)} %param.13) | copy-start | bytes 1572868
  0.6 71.3 %copy-start.1 = (f32[1,256,512]{2,1,0:T(8,128)S(1)}, f32[1,256,512]{2,1,0:T(8,128)}, u32[]{:S(2)}) copy-start(f32[1,256,512]{2,1,0:T(8,128)} %param.14) | copy-start | bytes 1572868
  0.7 71.3 %copy-start.2 = (f32[1,256,512]{2,1,0:T(8,128)S(1)}, f32[1,256,512]{2,1,0:T(8,128)}, u32[]{:S(2)}) copy-start(f32[1,256,512]{2,1,0:T(8,128)} %param.15) | copy-start | bytes 1572868
  0.7 71.3 %copy-start.3 = (f32[256,512]{1,0:T(8,128)S(1)}, f32[256,512]{1,0:T(8,128)}, u32[]{:S(2)}) copy-start(f32[256,512]{1,0:T(8,128)} %param.17) | copy-start | bytes 1572868
  0.7 71.3 %copy-start.4 = (f32[256,512]{1,0:T(8,128)S(1)}, f32[256,512]{1,0:T(8,128)}, u32[]{:S(2)}) copy-start(f32[256,512]{1,0:T(8,128)} %param.18) | copy-start | bytes 1572868

commit v3 on v2

--- a/solution.py
+++ b/solution.py
@@ -33,7 +33,7 @@
 def kernel(
     emb, pos_in, freq_in, cot, weight, pseudo,
     keyv, gout, dsum,
-    emba, wall, wf, cotv, psv, psb, kgt, ysend, yrecv, own, zs, zr, acc, accx,
+    emba, wall, wf, cotv, psv, psb, kgt, ysend, yrecv, own, zs, zr, acc, accs, accx,
     cosv, sinv, p1, p2s, p2r, pos, freq,
     loc, embl, embs, embr, kgs, kgr, ags, agr, yas, yar, yss, yrr, zss, zrr, xs, xr, p1ss, p1rr, p2ss, p2rr, p3ss, p3rr,
 ):
@@ -137,12 +137,15 @@
         cols = pl.multiple_of((2 * b + 1 - c) * ROWS, ROWS)
         return remote(emb.at[:, pl.ds(cols, ROWS)], emba.at[b, pl.ds(TOK, TOK)], embs.at[j], embr.at[j], twin)
 
-    def begin(j, _):
-        swap_emb(j).start()
+    def begin_load(j, _):
         load_emb(j).start()
         return 0
 
-    lax.fori_loop(0, 16, begin, 0)
+    def begin_swap(j, _):
+        swap_emb(j).start()
+        return 0
+
+    lax.fori_loop(0, 16, begin_load, 0)
     load_p.start()
 
     lane = lax.broadcasted_iota(jnp.int32, (192, 128), 1)
@@ -173,9 +176,11 @@
     tables(0)
     load_c.wait()
     back(0)
+    lax.fori_loop(0, 2, begin_swap, 0)
     swap_t.wait_recv()
     tables(1)
     swap_c.wait_recv()
+    lax.fori_loop(2, 4, begin_swap, 0)
     back(1)
 
     def block(j):
@@ -223,8 +228,10 @@
 
     far(0, 0)
     post_y(0)
+    lax.fori_loop(4, 6, begin_swap, 0)
     far(1, 0)
     post_y(1)
+    lax.fori_loop(6, 10, begin_swap, 0)
     enter(0)
     advance(0, 0)
 
@@ -242,6 +249,7 @@
         cp1.start()
 
     far(2, 0)
+    lax.fori_loop(10, 16, begin_swap, 0)
     lax.fori_loop(3, 5, far, 0)
     enter(1)
     advance(0, 1)
@@ -350,20 +358,15 @@
     products(6)
     relay(5, 0, 3, 1)
     relay(5, 0, 3, 0)
+    relay(6, 1, 3, 0)
+    relay(6, 1, 3, 1)
     advance(7, 0)
     advance(7, 1)
     products(7)
 
-    give_x = remote(acc.at[pl.ds(TOK, TOK)], accx, xs.at[0], xr.at[0], twin)
+    accs[...] = acc[TOK : 2 * TOK, :].astype(BF16)
+    give_x = remote(accs, accx, xs.at[0], xr.at[0], twin)
     give_x.start()
-    relay(6, 1, 3, 0)
-    relay(6, 1, 3, 1)
-    give_x.wait_recv()
-    for h in range(KV_HEADS):
-        at = slice(h * HD, (h + 1) * HD)
-        plain = acc[0:TOK, at] + accx[:, at]
-        keyv[:, at] = (plain * cosv[0] + pltpu.roll(plain, 64, 1) * sinv[0]).astype(BF16)
-
     for h in (0, 1):
         rows = pl.ds(h * HALF, HALF)
         total = here(7, h)
@@ -371,6 +374,12 @@
             hand(way, 3, h).wait_recv()
             total = total + zr[way, 3, rows, :].astype(F32)
         gout[:, h * HALF : (h + 1) * HALF] = jnp.transpose(total)
+
+    give_x.wait_recv()
+    for h in range(KV_HEADS):
+        at = slice(h * HD, (h + 1) * HD)
+        plain = acc[0:TOK, at] + accx[:, at].astype(F32)
+        keyv[:, at] = (plain * cosv[0] + pltpu.roll(plain, 64, 1) * sinv[0]).astype(BF16)
 
     for h in (0, 1):
         cross(h, mine).wait_send()
@@ -432,7 +441,8 @@
             pltpu.VMEM((2, 4, KW, ROWS), BF16),
             pltpu.VMEM((2, 4, KW, ROWS), BF16),
             pltpu.VMEM((2 * TOK, KW), F32),
-            pltpu.VMEM((TOK, KW), F32),
+            pltpu.VMEM((TOK, KW), BF16),
+            pltpu.VMEM((TOK, KW), BF16),
             pltpu.VMEM((2, TOK, HD), F32),
             pltpu.VMEM((2, TOK, HD), F32),
             pltpu.VMEM((3, 64, KW), BF16),
@@ -470,11 +480,58 @@
     )(*(pltpu.with_memory_space_constraint(v, pltpu.HBM) for v in operands))
 
 
-def outer_update(delta_sum, count, anchor_rows, momentum_rows):
-    mean_delta = delta_sum / count
-    momentum_next = 0.9 * momentum_rows + mean_delta
-    anchor_next = anchor_rows - 0.7 * (mean_delta + 0.9 * momentum_next)
-    return (anchor_next, momentum_next)
+def finish_kernel(
+    grad, delta, keys, weight, first, second, anchor, momentum,
+    keys_out, merged_out, first_out, second_out, anchor_out, momentum_out,
+    merged_v, first_v, second_v, anchor_v, momentum_v, sems,
+):
+    save_k = pltpu.make_async_copy(keys, keys_out, sems.at[0])
+    save_k.start()
+    saves = [save_k]
+
+    def save(src, dst, h):
+        rows = pl.ds(h * 128, 128)
+        copy = pltpu.make_async_copy(src.at[rows], dst.at[rows], sems.at[len(saves)])
+        copy.start()
+        saves.append(copy)
+
+    for h in (0, 1):
+        at = slice(h * 128, (h + 1) * 128)
+        mean_delta = delta[at, :].astype(F32) / 8
+        momentum_next = 0.9 * momentum[at, :] + mean_delta
+        anchor_next = anchor[at, :] - 0.7 * (mean_delta + 0.9 * momentum_next)
+        momentum_v[at, :] = momentum_next
+        anchor_v[at, :] = anchor_next
+        save(momentum_v, momentum_out, h)
+        save(anchor_v, anchor_out, h)
+        slope = grad[at, :]
+        first_next = 0.9 * first[at, :] + 0.1 * slope
+        second_next = 0.999 * second[at, :] + 0.001 * slope * slope
+        first_v[at, :] = first_next
+        second_v[at, :] = second_next
+        save(first_v, first_out, h)
+        save(second_v, second_out, h)
+        held = weight[at, :]
+        stepped = held - 0.001 * (first_next / (jnp.sqrt(second_next) + 1e-08) + 0.1 * held)
+        merged_v[at, :] = 0.5 * anchor_next + 0.5 * stepped
+        save(merged_v, merged_out, h)
+    for copy in saves:
+        copy.wait()
+
+
+def finish(*operands):
+    vmem_spec = pl.BlockSpec(memory_space=pltpu.VMEM)
+    any_spec = pl.BlockSpec(memory_space=pl.ANY)
+    block = jax.ShapeDtypeStruct((ROWS, KW), F32)
+    return pl.pallas_call(
+        finish_kernel,
+        out_shape=(jax.ShapeDtypeStruct((TOK, KW), BF16), *[block] * 5),
+        in_specs=[vmem_spec] * 8,
+        out_specs=(any_spec,) * 6,
+        scratch_shapes=[*[pltpu.VMEM((ROWS, KW), F32)] * 5, pltpu.SemaphoreType.DMA((11,))],
+        compiler_params=pltpu.CompilerParams(vmem_limit_bytes=8 * 1024 * 1024),
+        cost_estimate=pl.CostEstimate(flops=4 << 20, bytes_accessed=6 << 20, transcendentals=0),
+    )(*operands)
 
 
 def local(
@@ -490,12 +547,9 @@
 ):
     weight = local_weight[0]
     keys, grad, delta = step(embedded[0], positions, key_cotangent[0], weight, pseudo_grad[0])
-    first = 0.9 * adam_first[0] + 0.1 * grad
-    second = 0.999 * adam_second[0] + 0.001 * grad * grad
-    stepped = weight - 0.001 * (first / (jnp.sqrt(second) + 1e-08) + 0.1 * weight)
-    replicas = lax.axis_size("replica")
-    anchor_next, momentum_next = outer_update(delta.astype(F32), replicas, anchor, momentum)
-    merged = 0.5 * anchor_next + 0.5 * stepped
+    keys, merged, first, second, anchor_next, momentum_next = finish(
+        grad, delta, keys, weight, adam_first[0], adam_second[0], anchor, momentum
+    )
     return (keys[None], merged[None], first[None], second[None], anchor_next, momentum_next)
 
 

time: 74.5 us -> 72.9 us (0.979)
  other arithmetic: 1.69 us -> 0 us
  Pallas kernels: 71.2 us -> 72.1 us
  local copies, waits for them, and re-layouts: 0.77 us -> 0.02 us
    pallas_call x0 -> x1, Pallas kernels: none -> 1.71 us  [finish(): pl.pallas_call(finish_kernel, out_shape=(jax.ShapeDtypeStruct((TOK, KW),...]
    broadcast_in_dim x1 -> x0, other arithmetic: 1.69 us -> none  [local(): merged[None]]
    pallas_call x1, Pallas kernels: 71.2 us -> 70.4 us  [step(): pl.pallas_call(kernel, out_shape=(jax.ShapeDtypeStruct((TOK, KW), BF16),...]
    unnamed x11 -> x10, local copies, waits for them, and re-layouts: 0.77 us -> 0.02 us
where the time goes in v3:
time: 72.9 us
  Pallas kernels  72.1 us (99%)
    pallas_call x1, Pallas kernels, step(): pl.pallas_call(kernel, out_shape=(jax.ShapeDtypeStruct((TOK, KW), BF16),...  70.4 us
    pallas_call x1, Pallas kernels, finish(): pl.pallas_call(finish_kernel, out_shape=(jax.ShapeDtypeStruct((TOK, KW),...  1.71 us

profile of v3, /device:TPU:1, one launch (start us, length us, event | category | flops | bytes accessed | tf_op | source)
XLA Modules:
  0.0 72.9 jit_solution(3459644953954099070)
XLA Ops:
  0.6 0.0 copy-start
  0.6 0.0 copy-start.1
  0.7 0.0 copy-start.2
  0.7 0.0 copy-start.3
  0.7 0.0 copy-start.4
  0.7 70.4 %shard_map.145 = (bf16[384,512]{1,0:T(8,128)(2,1)S(1)}, f32[256,512]{1,0:T(8,128)S(1)}, bf16[256,512]{1,0:T(8,128)(2,1)S(1)}) custom-call(bf16[384,8192]{1,0:T(8,128)(2,1)} %bitcast.14, s32[1,384]{1,0:T(1,128)} %pos_in.1, f32[1,128]{1,0:T(1,128)} %constant.2.clone.freq_in, bf16[384,512]{1,0:T(8,128)(2,1)} %bitcast.19, f32[256,512]{1,0:T(8,128)} %bitcast.10, ...), custom_call_target="tpu_custom_call" | custom-call | flops 6442450944 | bytes 10485760 | tf_op jit(solution)/shard_map/pallas_call | solution.py:421
  71.1 0.0 copy-done
  71.1 0.0 copy-done.1
  71.1 0.0 copy-done.2
  71.1 0.0 copy-done.3
  71.1 0.0 copy-done.4
  71.1 1.7 %shard_map.146 = (bf16[384,512]{1,0:T(8,128)(2,1)}, f32[256,512]{1,0:T(8,128)}, f32[256,512]{1,0:T(8,128)}, f32[256,512]{1,0:T(8,128)}, f32[256,512]{1,0:T(8,128)}, /*index=5*/f32[256,512]{1,0:T(8,128)}) custom-call(f32[256,512]{1,0:T(8,128)S(1)} %get-tuple-element.15.grad, bf16[256,512]{1,0:T(8,128)(2,1)S(1)} %get-tuple-element.16.delta, ...), custom_call_target="tpu_custom_call" | custom-call | flops 4194304 | bytes 6291456 | tf_op jit(solution)/shard_map/pallas_call | solution.py:526
Async XLA Ops:
  0.6 70.5 %copy-start = (f32[1,256,512]{2,1,0:T(8,128)S(1)}, f32[1,256,512]{2,1,0:T(8,128)}, u32[]{:S(2)}) copy-start(f32[1,256,512]{2,1,0:T(8,128)} %param.13) | copy-start | bytes 1572868
  0.6 70.5 %copy-start.1 = (f32[1,256,512]{2,1,0:T(8,128)S(1)}, f32[1,256,512]{2,1,0:T(8,128)}, u32[]{:S(2)}) copy-start(f32[1,256,512]{2,1,0:T(8,128)} %param.14) | copy-start | bytes 1572868
  0.7 70.5 %copy-start.2 = (f32[1,256,512]{2,1,0:T(8,128)S(1)}, f32[1,256,512]{2,1,0:T(8,128)}, u32[]{:S(2)}) copy-start(f32[1,256,512]{2,1,0:T(8,128)} %param.15) | copy-start | bytes 1572868
  0.7 70.5 %copy-start.3 = (f32[256,512]{1,0:T(8,128)S(1)}, f32[256,512]{1,0:T(8,128)}, u32[]{:S(2)}) copy-start(f32[256,512]{1,0:T(8,128)} %anchor.1) | copy-start | bytes 1572868
  0.7 70.5 %copy-start.4 = (f32[256,512]{1,0:T(8,128)S(1)}, f32[256,512]{1,0:T(8,128)}, u32[]{:S(2)}) copy-start(f32[256,512]{1,0:T(8,128)} %momentum.1) | copy-start | bytes 1572868

commit v4 on v3

--- a/solution.py
+++ b/solution.py
@@ -17,7 +17,7 @@
 ROWS = 256
 KW = 512
 HALF = 256
-HOP = 64
+HOP = 48
 AHEAD = 2
 MESH = pl.DeviceIdType.MESH
 F32 = jnp.float32
@@ -257,7 +257,7 @@
     lax.fori_loop(0, 8, near, 0)
     advance(1, 0)
 
-    def product(b, first=False):
+    def product(b, first=False, begin=0, end=3):
         def part(m, _):
             at = pl.ds(pl.multiple_of(m * 256, 256), 256)
             value = jnp.dot(emba[b, at, :], wall[b], preferred_element_type=F32)
@@ -267,7 +267,7 @@
                 acc[at, :] += value
             return 0
 
-        lax.fori_loop(0, 3, part, 0)
+        lax.fori_loop(begin, end, part, 0)
 
     def products(k):
         d, p = k // 2, k % 2
@@ -362,11 +362,12 @@
     relay(6, 1, 3, 1)
     advance(7, 0)
     advance(7, 1)
-    products(7)
+    product(slot(z - 4, 1 - yh), begin=1)
 
     accs[...] = acc[TOK : 2 * TOK, :].astype(BF16)
     give_x = remote(accs, accx, xs.at[0], xr.at[0], twin)
     give_x.start()
+    product(slot(z - 4, 1 - yh), end=1)
     for h in (0, 1):
         rows = pl.ds(h * HALF, HALF)
         total = here(7, h)

time: 72.9 us -> 72.8 us (level)
  no operation moved by 1% of the time
where the time goes in v4:
time: 72.8 us; the launch traced here: 72.4 us
  Pallas kernels  71.7 us (98%)
    pallas_call x1, Pallas kernels, step(): pl.pallas_call(kernel, out_shape=(jax.ShapeDtypeStruct((TOK, KW), BF16),...  69.9 us
    pallas_call x1, Pallas kernels, finish(): pl.pallas_call(finish_kernel, out_shape=(jax.ShapeDtypeStruct((TOK, KW),...  1.71 us

profile of v4, /device:TPU:1, one launch (start us, length us, event | category | flops | bytes accessed | tf_op | source)
XLA Modules:
  0.0 72.4 jit_solution(352764520992769155)
XLA Ops:
  0.6 0.0 copy-start
  0.6 0.0 copy-start.1
  0.7 0.0 copy-start.2
  0.7 0.0 copy-start.3
  0.7 0.0 copy-start.4
  0.7 69.9 %shard_map.145 = (bf16[384,512]{1,0:T(8,128)(2,1)S(1)}, f32[256,512]{1,0:T(8,128)S(1)}, bf16[256,512]{1,0:T(8,128)(2,1)S(1)}) custom-call(bf16[384,8192]{1,0:T(8,128)(2,1)} %bitcast.14, s32[1,384]{1,0:T(1,128)} %pos_in.1, f32[1,128]{1,0:T(1,128)} %constant.2.clone.freq_in, bf16[384,512]{1,0:T(8,128)(2,1)} %bitcast.19, f32[256,512]{1,0:T(8,128)} %bitcast.10, ...), custom_call_target="tpu_custom_call" | custom-call | flops 6442450944 | bytes 10485760 | tf_op jit(solution)/shard_map/pallas_call | solution.py:422
  70.6 0.0 copy-done
  70.7 0.0 copy-done.1
  70.7 0.0 copy-done.2
  70.7 0.0 copy-done.3
  70.7 0.0 copy-done.4
  70.7 1.7 %shard_map.146 = (bf16[384,512]{1,0:T(8,128)(2,1)}, f32[256,512]{1,0:T(8,128)}, f32[256,512]{1,0:T(8,128)}, f32[256,512]{1,0:T(8,128)}, f32[256,512]{1,0:T(8,128)}, /*index=5*/f32[256,512]{1,0:T(8,128)}) custom-call(f32[256,512]{1,0:T(8,128)S(1)} %get-tuple-element.15.grad, bf16[256,512]{1,0:T(8,128)(2,1)S(1)} %get-tuple-element.16.delta, ...), custom_call_target="tpu_custom_call" | custom-call | flops 4194304 | bytes 6291456 | tf_op jit(solution)/shard_map/pallas_call | solution.py:527
Async XLA Ops:
  0.6 70.0 %copy-start = (f32[1,256,512]{2,1,0:T(8,128)S(1)}, f32[1,256,512]{2,1,0:T(8,128)}, u32[]{:S(2)}) copy-start(f32[1,256,512]{2,1,0:T(8,128)} %param.13) | copy-start | bytes 1572868
  0.6 70.0 %copy-start.1 = (f32[1,256,512]{2,1,0:T(8,128)S(1)}, f32[1,256,512]{2,1,0:T(8,128)}, u32[]{:S(2)}) copy-start(f32[1,256,512]{2,1,0:T(8,128)} %param.14) | copy-start | bytes 1572868
  0.7 70.0 %copy-start.2 = (f32[1,256,512]{2,1,0:T(8,128)S(1)}, f32[1,256,512]{2,1,0:T(8,128)}, u32[]{:S(2)}) copy-start(f32[1,256,512]{2,1,0:T(8,128)} %param.15) | copy-start | bytes 1572868
  0.7 70.0 %copy-start.3 = (f32[256,512]{1,0:T(8,128)S(1)}, f32[256,512]{1,0:T(8,128)}, u32[]{:S(2)}) copy-start(f32[256,512]{1,0:T(8,128)} %anchor.1) | copy-start | bytes 1572868
  0.7 70.0 %copy-start.4 = (f32[256,512]{1,0:T(8,128)S(1)}, f32[256,512]{1,0:T(8,128)}, u32[]{:S(2)}) copy-start(f32[256,512]{1,0:T(8,128)} %momentum.1) | copy-start | bytes 1572868
